TPU v7x, 32 devices: a whole 2x2x4 slice. The times are simulated.
32 devices in a mesh: gz: 4 (over z), gy: 4 (over x, core), col: 2 (over y).
Axes of the slice: x: 2, y: 2, z: 4, core: 2. Of those that a mesh axis runs over, the one named last changes fastest.
Arguments:
- volume: bfloat16 [8, 8, 1024, 128], P('gz', 'gy', 'col'), may hold values from -6 to 6
- conv_weight: bfloat16 [27, 2, 1024, 1024], P(None, None, 'col'), may hold values from -0.0390625 to 0.0390625
- proj_weight: bfloat16 [1024, 512], replicated, may hold values from -0.1875 to 0.1875
Outputs:
- fine_tiles: float32 [32, 32, 4096], P('gz', 'gy', 'col')
All inputs are finite; a program needn't handle non-finite values.
Results may differ from a plain program's by a relative error of at most 0.0029.
Values may be sent and summed in bfloat16 or wider, within the bound.
A program may use at most 128 MiB of HBM per device.

v0:
```python
import jax
import jax.numpy as jnp
from jax import lax
from jax.sharding import PartitionSpec as P


def extended_2(cells, sides, width, closed):
    for axis, dim in sides:
        count = lax.axis_size(axis)
        ends = count if closed else count - 1
        head = lax.slice_in_dim(cells, 0, width, axis=dim)
        tail = lax.slice_in_dim(cells, cells.shape[dim] - width, cells.shape[dim], axis=dim)
        cells = jnp.concatenate(
            [
                lax.ppermute(tail, axis, [(i, (i + 1) % count) for i in range(ends)]),
                cells,
                lax.ppermute(head, axis, [((i + 1) % count, i) for i in range(ends)]),
            ],
            axis=dim,
        )
    return cells


def inverse_lift(low_band, high_band, along):
    length = low_band.shape[along]

    def window_of(array, first, last):
        return lax.slice_in_dim(array, first, last, axis=along)

    even_rows = window_of(low_band, 1, length - 1) - 0.25 * (
        window_of(high_band, 0, length - 2) + window_of(high_band, 1, length - 1)
    )
    next_even = window_of(low_band, 2, length) - 0.25 * (
        window_of(high_band, 1, length - 1) + window_of(high_band, 2, length)
    )
    odd_rows = window_of(high_band, 1, length - 1) + 0.5 * (even_rows + next_even)
    paired = jnp.stack([even_rows, odd_rows], axis=along + 1)
    new_shape = list(even_rows.shape)
    new_shape[along] = 2 * (length - 2)
    return paired.reshape(new_shape)


def synthesize(coefficients):
    quarter = coefficients.shape[-1] // 4
    bands = coefficients.reshape(coefficients.shape[:-1] + (4, quarter))
    low_z = inverse_lift(bands[..., 0, :], bands[..., 2, :], 0)
    high_z = inverse_lift(bands[..., 1, :], bands[..., 3, :], 0)
    return inverse_lift(low_z, high_z, 1)


def convolve(brick_data, tap_weights):
    kernel = tap_weights.reshape(
        (3, 3, 3, tap_weights.shape[1] * tap_weights.shape[2], tap_weights.shape[3])
    )
    result = lax.conv_general_dilated(
        brick_data[None],
        kernel,
        (1, 1, 1),
        ((0, 0), (0, 0), (1, 1)),
        dimension_numbers=("NDHCW", "DHWOI", "NDHCW"),
        preferred_element_type=jnp.float32,
    )
    return result[0]


def on_device(volume, conv_weight, proj_weight):
    out_width = conv_weight.shape[2]
    gathered = lax.all_gather(volume, "col", axis=2, tiled=True)
    extended = extended_2(gathered, (("gz", 0), ("gy", 1)), 1, False)
    conv_out = convolve(extended, conv_weight)
    gated_values = (
        jax.nn.silu(conv_out[:, :, :out_width, :]) * conv_out[:, :, out_width:, :]
    ).astype(jnp.bfloat16)
    coefficients = jnp.einsum(
        "zycx,cp->zyxp",
        lax.all_to_all(gated_values, "col", split_axis=3, concat_axis=2, tiled=True),
        proj_weight,
        preferred_element_type=jnp.float32,
    )
    coarse = extended_2(coefficients, (("gz", 0), ("gy", 1)), 1, True)
    middle = synthesize(coarse)
    middle_rims = extended_2(middle, (("gz", 0), ("gy", 1)), 1, True)
    fine_tiles = synthesize(middle_rims)
    return fine_tiles.reshape(
        (fine_tiles.shape[0], fine_tiles.shape[1], fine_tiles.shape[2] * fine_tiles.shape[3])
    )


def solution(mesh):
    return jax.shard_map(
        on_device,
        mesh=mesh,
        in_specs=(P("gz", "gy", "col", None), P(None, None, "col", None), P()),
        out_specs=P("gz", "gy", "col"),
        check_vma=False,
    )
```

profile of v0, /device:TPU:1, one launch (start us, length us, event | category | flops | bytes accessed | tf_op | source)
XLA Modules:
  0.0 203.0 jit_solution(1230843944863222755)
XLA Ops:
  7.3 25.1 %all-gather.2.cloned.1.call-done = bf16[2,2,1024,128]{3,2,1,0:T(8,128)(2,1)} async-done(((bf16[2,2,512,128]{3,2,1,0:T(8,128)(2,1)}), bf16[2,2,1024,128]{3,2,1,0:T(8,128)(2,1)}) %all-gather.2.cloned.1.call-update) | async-done | bytes 1048592 | tf_op jit(solution)/shard_map/all_gather | solution.py:68
  33.7 3.1 %collective-permute-start = (bf16[1,2,1024,128]{3,2,1,0:T(8,128)(2,1)S(1)}, bf16[1,2,1024,128]{3,2,1,0:T(8,128)(2,1)S(1)}, u32[]{:S(2)}, u32[]{:S(2)}) collective-permute-start(bf16[1,2,1024,128]{3,2,1,0:T(8,128)(2,1)S(1)} %get-tuple-element.34), channel_id=1, source_target_pairs={{0,8},{8,16},{16,24},{1,9},{9,17},{17,25},{2,10},{10,18},{18,26},{... | collective-permute-start | bytes 1572872 | tf_op jit(solution)/shard_map/ppermute | solution.py:15
  38.1 9.2 %collective-permute-done = bf16[1,2,1024,128]{3,2,1,0:T(8,128)(2,1)S(1)} collective-permute-done((bf16[1,2,1024,128]{3,2,1,0:T(8,128)(2,1)S(1)}, bf16[1,2,1024,128]{3,2,1,0:T(8,128)(2,1)S(1)}, u32[]{:S(2)}, u32[]{:S(2)}) %collective-permute-start) | collective-permute-done | bytes 524320 | tf_op jit(solution)/shard_map/ppermute | solution.py:15
  47.6 3.6 %collective-permute-done.1 = bf16[1,2,1024,128]{3,2,1,0:T(8,128)(2,1)S(1)} collective-permute-done((bf16[1,2,1024,128]{3,2,1,0:T(8,128)(2,1)S(1)}, bf16[1,2,1024,128]{3,2,1,0:T(8,128)(2,1)S(1)}, u32[]{:S(2)}, u32[]{:S(2)}) %collective-permute-start.1) | collective-permute-done | bytes 524320 | tf_op jit(solution)/shard_map/ppermute | solution.py:17
  51.4 4.8 %collective-permute-start.2 = (bf16[4,1,1024,128]{3,2,1,0:T(8,128)(2,1)S(1)}, bf16[4,1,1024,128]{3,2,1,0:T(8,128)(2,1)S(1)}, u32[]{:S(2)}, u32[]{:S(2)}) collective-permute-start(bf16[4,1,1024,128]{3,2,1,0:T(8,128)(2,1)S(1)} %get-tuple-element.25), channel_id=1, source_target_pairs={{0,2},{2,4},{4,6},{1,3},{3,5},{5,7},{8,10},{10,12},{12,14},{9,11},... | collective-permute-start | bytes 3145736 | tf_op jit(solution)/shard_map/ppermute | solution.py:15
  56.3 1.9 collective-permute-start.3
  58.2 9.8 %collective-permute-done.2 = bf16[4,1,1024,128]{3,2,1,0:T(8,128)(2,1)S(1)} collective-permute-done((bf16[4,1,1024,128]{3,2,1,0:T(8,128)(2,1)S(1)}, bf16[4,1,1024,128]{3,2,1,0:T(8,128)(2,1)S(1)}, u32[]{:S(2)}, u32[]{:S(2)}) %collective-permute-start.2) | collective-permute-done | bytes 1048608 | tf_op jit(solution)/shard_map/ppermute | solution.py:15
  68.0 4.4 %collective-permute-done.3 = bf16[4,1,1024,128]{3,2,1,0:T(8,128)(2,1)S(1)} collective-permute-done((bf16[4,1,1024,128]{3,2,1,0:T(8,128)(2,1)S(1)}, bf16[4,1,1024,128]{3,2,1,0:T(8,128)(2,1)S(1)}, u32[]{:S(2)}, u32[]{:S(2)}) %collective-permute-start.3) | collective-permute-done | bytes 1048608 | tf_op jit(solution)/shard_map/ppermute | solution.py:17
  72.4 2.2 %maximum_bitcast_fusion = bf16[4,4,1024,1,128]{4,2,1,0,3:T(8,128)(2,1)} fusion(bf16[4,1,1024,128]{3,2,1,0:T(8,128)(2,1)S(1)} %collective-permute-done.3, bf16[4,2,1024,128]{3,2,1,0:T(8,128)(2,1)S(1)} %constant_dynamic-update-slice_fusion, bf16[4,1,1024,128]{3,2,1,0:T(8,128)(2,1)S(1)} %collective-permute-done.2), kind=kLoop, calls=%fused_computation.8 | loop fusion | flops 4194304 | bytes 8388608 | tf_op jit(solution)/shard_map/broadcast_in_dim | solution.py:56
  74.6 7.9 %copy.172 = bf16[4,4,1024,1,128]{2,1,4,0,3:T(4,128)(2,1)} copy(bf16[4,4,1024,1,128]{4,2,1,0,3:T(8,128)(2,1)} %maximum_bitcast_fusion) | data formatting | bytes 8388608
  82.5 3.9 %pad.clone = bf16[4,4,1024,1,136]{2,1,4,0,3:T(4,128)(2,1)S(1)} pad(bf16[4,4,1024,1,128]{2,1,4,0,3:T(4,128)(2,1)} %copy.172, bf16[]{:T(256)} %constant.2), padding=0_0x0_0x0_0x0_0x1_7 | pad | bytes 8650754 | tf_op jit(solution)/shard_map/broadcast_in_dim | solution.py:56
  86.4 1.5 copy.119
  88.1 37.2 %fusion.9 = f32[2,2,8,17,1024]{4,2,3,1,0:T(8,128)S(1)} fusion(bf16[3,3,3,1024,1024]{4,3,2,1,0:T(8,128)(2,1)} %bitcast.195, bf16[4,4,1024,1,7,2]{2,4,5,1,0,3:T(8,128)(2,1)S(1)} %slice.310, bf16[4,4,1024,1,8,17]{2,4,5,1,0,3:T(8,128)(2,1)S(1)} %copy.119, pred[8,17]{0,1:T(8,128)(4,1)S(1)} %copy-done.2), kind=kOutput, calls=%fused_computation.11 | convolution fusion | flops 30818467840 | bytes 63766664 | tf_op jit(solution)/shard_map/conv_general_dilated | solution.py:55
  125.3 1.7 copy.120
  127.0 2.1 %slice.311 = f32[2,2,1,128,1024]{4,1,3,0,2:T(2,128)} slice(f32[2,2,1,136,1024]{4,1,3,0,2:T(2,128)S(1)} %bitcast.173), slice={[0:2], [0:2], [0:1], [0:128], [0:1024]} | slice | bytes 4194304 | tf_op jit(solution)/shard_map/conv_general_dilated | solution.py:55
  129.1 2.8 %copy.152 = f32[2,2,1,128,1024]{3,4,1,0,2:T(8,128)S(1)} copy(f32[2,2,1,128,1024]{4,1,3,0,2:T(2,128)} %slice.311) | data formatting | bytes 4194304
  134.3 8.1 %all_to_all.18 = bf16[2,2,512,128]{2,1,0,3:T(2,128)(2,1)S(1)} all-to-all(bf16[2,2,512,128]{2,1,0,3:T(2,128)(2,1)S(1)} %copy.122), channel_id=1, replica_groups=mesh['gz'=4,'gy'=4,'col'=2] {'col'}, dimensions={3} | all-to-all | bytes 1048576 | tf_op jit(solution)/shard_map/all_to_all | solution.py:76
  144.1 2.4 %collective-permute-start.5 = (f32[1,2,64,512]{3,2,1,0:T(8,128)S(1)}, f32[1,2,64,512]{3,2,1,0:T(8,128)S(1)}, u32[]{:S(2)}, u32[]{:S(2)}) collective-permute-start(f32[1,2,64,512]{3,2,1,0:T(8,128)S(1)} %get-tuple-element.40), channel_id=1, source_target_pairs={{8,0},{16,8},{24,16},{0,24},{9,1},{17,9},{25,17},{1,25},{10,2},{18... | collective-permute-start | bytes 786440 | tf_op jit(solution)/shard_map/ppermute | solution.py:17
  146.4 3.9 %collective-permute-done.4 = f32[1,2,64,512]{3,2,1,0:T(8,128)S(1)} collective-permute-done((f32[1,2,64,512]{3,2,1,0:T(8,128)S(1)}, f32[1,2,64,512]{3,2,1,0:T(8,128)S(1)}, u32[]{:S(2)}, u32[]{:S(2)}) %collective-permute-start.4) | collective-permute-done | bytes 262176 | tf_op jit(solution)/shard_map/ppermute | solution.py:15
  150.4 1.7 collective-permute-done.5
  152.2 2.5 %collective-permute-start.6 = (f32[4,1,64,512]{3,2,1,0:T(8,128)S(1)}, f32[4,1,64,512]{3,2,1,0:T(8,128)S(1)}, u32[]{:S(2)}, u32[]{:S(2)}) collective-permute-start(f32[4,1,64,512]{3,2,1,0:T(8,128)S(1)} %get-tuple-element.31), channel_id=1, source_target_pairs={{0,2},{2,4},{4,6},{6,0},{1,3},{3,5},{5,7},{7,1},{8,10},{10,12},{12... | collective-permute-start | bytes 1572872 | tf_op jit(solution)/shard_map/ppermute | solution.py:15
  154.7 10.0 %collective-permute-done.6 = f32[4,1,64,512]{3,2,1,0:T(8,128)S(1)} collective-permute-done((f32[4,1,64,512]{3,2,1,0:T(8,128)S(1)}, f32[4,1,64,512]{3,2,1,0:T(8,128)S(1)}, u32[]{:S(2)}, u32[]{:S(2)}) %collective-permute-start.6) | collective-permute-done | bytes 524320 | tf_op jit(solution)/shard_map/ppermute | solution.py:15
  166.3 1.9 reshape.391
  168.2 2.4 %fusion.58 = (f32[2,4,64,1,128]{4,3,2,1,0:T(1,128)S(1)}, f32[2,4,64,1,128]{4,3,2,1,0:T(1,128)S(1)}, f32[2,4,64,1,128]{4,3,2,1,0:T(1,128)S(1)}, f32[2,4,64,1,128]...) fusion(f32[4,4,64,4,128]{4,3,2,1,0:T(4,128)S(1)} %reshape.391), kind=kLoop, calls=%fused_computation.93 | loop fusion | bytes 5242880 | tf_op jit(solution)/shard_map/slice | solution.py:28
  171.1 1.9 collective-permute-start.9
  173.1 3.2 %collective-permute-done.9 = f32[1,4,64,128]{3,2,1,0:T(8,128)S(1)} collective-permute-done((f32[1,4,64,128]{3,2,1,0:T(8,128)S(1)}, f32[1,4,64,128]{3,2,1,0:T(8,128)S(1)}, u32[]{:S(2)}, u32[]{:S(2)}) %collective-permute-start.9) | collective-permute-done | bytes 131104 | tf_op jit(solution)/shard_map/ppermute | solution.py:17
  176.3 3.7 %collective-permute-done.8 = f32[1,4,64,128]{3,2,1,0:T(8,128)S(1)} collective-permute-done((f32[1,4,64,128]{3,2,1,0:T(8,128)S(1)}, f32[1,4,64,128]{3,2,1,0:T(8,128)S(1)}, u32[]{:S(2)}, u32[]{:S(2)}) %collective-permute-start.8) | collective-permute-done | bytes 131104 | tf_op jit(solution)/shard_map/ppermute | solution.py:15
  180.0 2.6 %collective-permute-start.10 = (f32[6,1,64,128]{3,2,1,0:T(8,128)S(1)}, f32[6,1,64,128]{3,2,1,0:T(8,128)S(1)}, u32[]{:S(2)}, u32[]{:S(2)}) collective-permute-start(f32[6,1,64,128]{3,2,1,0:T(8,128)S(1)} %get-tuple-element.35), channel_id=1, source_target_pairs={{0,2},{2,4},{4,6},{6,0},{1,3},{3,5},{5,7},{7,1},{8,10},{10,12},{12... | collective-permute-start | bytes 589832 | tf_op jit(solution)/shard_map/ppermute | solution.py:15
  182.6 4.5 %collective-permute-done.10 = f32[6,1,64,128]{3,2,1,0:T(8,128)S(1)} collective-permute-done((f32[6,1,64,128]{3,2,1,0:T(8,128)S(1)}, f32[6,1,64,128]{3,2,1,0:T(8,128)S(1)}, u32[]{:S(2)}, u32[]{:S(2)}) %collective-permute-start.10) | collective-permute-done | bytes 196640 | tf_op jit(solution)/shard_map/ppermute | solution.py:15
  188.8 1.8 copy.138
  192.5 1.8 copy.150
  194.4 1.7 reshape_reshape.3
  (48 shorter events, 13.6 us)
Async XLA Ops:
  6.5 136.1 %copy-start = (bf16[1024,512]{1,0:T(8,128)(2,1)S(1)}, bf16[1024,512]{1,0:T(8,128)(2,1)}, u32[]{:S(2)}) copy-start(bf16[1024,512]{1,0:T(8,128)(2,1)} %param.5) | copy-start | bytes 3145732
  6.5 25.8 %all-gather.2.cloned.1.call-start = ((), (), s32[]{:S(2)}) async-start(), calls=%async_computation.1 | async-start | bytes 1572864 | tf_op jit(solution)/shard_map/all_gather | solution.py:68
  32.3 15.1 %copy-start.1 = (bf16[2,2,1024,128]{3,2,1,0:T(8,128)(2,1)S(1)}, bf16[2,2,1024,128]{3,2,1,0:T(8,128)(2,1)}, u32[]{:S(2)}) copy-start(bf16[2,2,1024,128]{3,2,1,0:T(8,128)(2,1)} %all-gather.2.cloned.1.call-done) | copy-start | bytes 3145732
  33.7 13.7 %collective-permute-start = (bf16[1,2,1024,128]{3,2,1,0:T(8,128)(2,1)S(1)}, bf16[1,2,1024,128]{3,2,1,0:T(8,128)(2,1)S(1)}, u32[]{:S(2)}, u32[]{:S(2)}) collective-permute-start(bf16[1,2,1024,128]{3,2,1,0:T(8,128)(2,1)S(1)} %get-tuple-element.34), channel_id=1, source_target_pairs={{0,8},{8,16},{16,24},{1,9},{9,17},{17,25},{2,10},{10,18},{18,26},{... | collective-permute-start | bytes 1572872 | tf_op jit(solution)/shard_map/ppermute | solution.py:15
  36.8 14.4 %collective-permute-start.1 = (bf16[1,2,1024,128]{3,2,1,0:T(8,128)(2,1)S(1)}, bf16[1,2,1024,128]{3,2,1,0:T(8,128)(2,1)S(1)}, u32[]{:S(2)}, u32[]{:S(2)}) collective-permute-start(bf16[1,2,1024,128]{3,2,1,0:T(8,128)(2,1)S(1)} %get-tuple-element.33), channel_id=1, source_target_pairs={{8,0},{16,8},{24,16},{9,1},{17,9},{25,17},{10,2},{18,10},{26,18},{... | collective-permute-start | bytes 1572872 | tf_op jit(solution)/shard_map/ppermute | solution.py:17
  51.4 16.6 %collective-permute-start.2 = (bf16[4,1,1024,128]{3,2,1,0:T(8,128)(2,1)S(1)}, bf16[4,1,1024,128]{3,2,1,0:T(8,128)(2,1)S(1)}, u32[]{:S(2)}, u32[]{:S(2)}) collective-permute-start(bf16[4,1,1024,128]{3,2,1,0:T(8,128)(2,1)S(1)} %get-tuple-element.25), channel_id=1, source_target_pairs={{0,2},{2,4},{4,6},{1,3},{3,5},{5,7},{8,10},{10,12},{12,14},{9,11},... | collective-permute-start | bytes 3145736 | tf_op jit(solution)/shard_map/ppermute | solution.py:15
  56.3 16.1 %collective-permute-start.3 = (bf16[4,1,1024,128]{3,2,1,0:T(8,128)(2,1)S(1)}, bf16[4,1,1024,128]{3,2,1,0:T(8,128)(2,1)S(1)}, u32[]{:S(2)}, u32[]{:S(2)}) collective-permute-start(bf16[4,1,1024,128]{3,2,1,0:T(8,128)(2,1)S(1)} %get-tuple-element.26), channel_id=1, source_target_pairs={{2,0},{4,2},{6,4},{3,1},{5,3},{7,5},{10,8},{12,10},{14,12},{11,9},... | collective-permute-start | bytes 3145736 | tf_op jit(solution)/shard_map/ppermute | solution.py:17
  86.4 1.7 copy-start.2
  143.1 7.2 %collective-permute-start.4 = (f32[1,2,64,512]{3,2,1,0:T(8,128)S(1)}, f32[1,2,64,512]{3,2,1,0:T(8,128)S(1)}, u32[]{:S(2)}, u32[]{:S(2)}) collective-permute-start(f32[1,2,64,512]{3,2,1,0:T(8,128)S(1)} %get-tuple-element.39), channel_id=1, source_target_pairs={{0,8},{8,16},{16,24},{24,0},{1,9},{9,17},{17,25},{25,1},{2,10},{10... | collective-permute-start | bytes 786440 | tf_op jit(solution)/shard_map/ppermute | solution.py:15
  144.1 8.0 %collective-permute-start.5 = (f32[1,2,64,512]{3,2,1,0:T(8,128)S(1)}, f32[1,2,64,512]{3,2,1,0:T(8,128)S(1)}, u32[]{:S(2)}, u32[]{:S(2)}) collective-permute-start(f32[1,2,64,512]{3,2,1,0:T(8,128)S(1)} %get-tuple-element.40), channel_id=1, source_target_pairs={{8,0},{16,8},{24,16},{0,24},{9,1},{17,9},{25,17},{1,25},{10,2},{18... | collective-permute-start | bytes 786440 | tf_op jit(solution)/shard_map/ppermute | solution.py:17
  152.2 12.5 %collective-permute-start.6 = (f32[4,1,64,512]{3,2,1,0:T(8,128)S(1)}, f32[4,1,64,512]{3,2,1,0:T(8,128)S(1)}, u32[]{:S(2)}, u32[]{:S(2)}) collective-permute-start(f32[4,1,64,512]{3,2,1,0:T(8,128)S(1)} %get-tuple-element.31), channel_id=1, source_target_pairs={{0,2},{2,4},{4,6},{6,0},{1,3},{3,5},{5,7},{7,1},{8,10},{10,12},{12... | collective-permute-start | bytes 1572872 | tf_op jit(solution)/shard_map/ppermute | solution.py:15
  154.7 10.0 %collective-permute-start.7 = (f32[4,1,64,512]{3,2,1,0:T(8,128)S(1)}, f32[4,1,64,512]{3,2,1,0:T(8,128)S(1)}, u32[]{:S(2)}, u32[]{:S(2)}) collective-permute-start(f32[4,1,64,512]{3,2,1,0:T(8,128)S(1)} %get-tuple-element.32), channel_id=1, source_target_pairs={{2,0},{4,2},{6,4},{0,6},{3,1},{5,3},{7,5},{1,7},{10,8},{12,10},{14... | collective-permute-start | bytes 1572872 | tf_op jit(solution)/shard_map/ppermute | solution.py:17
  171.1 5.2 %collective-permute-start.9 = (f32[1,4,64,128]{3,2,1,0:T(8,128)S(1)}, f32[1,4,64,128]{3,2,1,0:T(8,128)S(1)}, u32[]{:S(2)}, u32[]{:S(2)}) collective-permute-start(f32[1,4,64,128]{3,2,1,0:T(8,128)S(1)} %bitcast.194), channel_id=1, source_target_pairs={{8,0},{16,8},{24,16},{0,24},{9,1},{17,9},{25,17},{1,25},{10,2},{18... | collective-permute-start | bytes 393224 | tf_op jit(solution)/shard_map/ppermute | solution.py:17
  173.0 7.0 %collective-permute-start.8 = (f32[1,4,64,128]{3,2,1,0:T(8,128)S(1)}, f32[1,4,64,128]{3,2,1,0:T(8,128)S(1)}, u32[]{:S(2)}, u32[]{:S(2)}) collective-permute-start(f32[1,4,64,128]{3,2,1,0:T(8,128)S(1)} %bitcast.193), channel_id=1, source_target_pairs={{0,8},{8,16},{16,24},{24,0},{1,9},{9,17},{17,25},{25,1},{2,10},{10... | collective-permute-start | bytes 393224 | tf_op jit(solution)/shard_map/ppermute | solution.py:15
  180.0 7.1 %collective-permute-start.10 = (f32[6,1,64,128]{3,2,1,0:T(8,128)S(1)}, f32[6,1,64,128]{3,2,1,0:T(8,128)S(1)}, u32[]{:S(2)}, u32[]{:S(2)}) collective-permute-start(f32[6,1,64,128]{3,2,1,0:T(8,128)S(1)} %get-tuple-element.35), channel_id=1, source_target_pairs={{0,2},{2,4},{4,6},{6,0},{1,3},{3,5},{5,7},{7,1},{8,10},{10,12},{12... | collective-permute-start | bytes 589832 | tf_op jit(solution)/shard_map/ppermute | solution.py:15
  182.6 5.1 %collective-permute-start.11 = (f32[6,1,64,128]{3,2,1,0:T(8,128)S(1)}, f32[6,1,64,128]{3,2,1,0:T(8,128)S(1)}, u32[]{:S(2)}, u32[]{:S(2)}) collective-permute-start(f32[6,1,64,128]{3,2,1,0:T(8,128)S(1)} %get-tuple-element.36), channel_id=1, source_target_pairs={{2,0},{4,2},{6,4},{0,6},{3,1},{5,3},{7,5},{1,7},{10,8},{12,10},{14... | collective-permute-start | bytes 589832 | tf_op jit(solution)/shard_map/ppermute | solution.py:17
Sparse Core Ops, SparseCore 0:
  8.9 23.3 all-gather.1
where the time goes:
time: 204 us; the launch traced here: 203 us
  waiting for transfers between devices  80.5 us (39%)
  matrix products  37.6 us (18%)
  local copies, waits for them, and re-layouts  33.4 us (16%)
  starting transfers between devices  21.4 us (10%)
  between operations  13.7 us (7%)
  blocking collectives  8.14 us (4%)
  other arithmetic  8.12 us (4%)
    ppermute x6, waiting for transfers between devices, extended_2(): lax.ppermute(tail, axis, [(i, (i + 1) % count) for i in range(ends)])  41.2 us
    conv_general_dilated x1, matrix products, convolve(): lax.conv_general_dilated(brick_data[None], kernel, (1, 1, 1), ((0, 0), (0...  37.2 us
    all_gather x1, waiting for transfers between devices, on_device(): gathered = lax.all_gather(volume, 'col', axis=2, tiled=True)  25.1 us
    ppermute x6, starting transfers between devices, extended_2(): lax.ppermute(tail, axis, [(i, (i + 1) % count) for i in range(ends)])  14 us
    ppermute x6, waiting for transfers between devices, extended_2(): lax.ppermute(head, axis, [((i + 1) % count, i) for i in range(ends)])  13.6 us
    unnamed x10, local copies, waits for them, and re-layouts  10.9 us
    all_to_all x1, blocking collectives, on_device(): lax.all_to_all(gated_values, 'col', split_axis=3, concat_axis=2, tiled=True)  8.14 us
    ppermute x6, starting transfers between devices, extended_2(): lax.ppermute(head, axis, [((i + 1) % count, i) for i in range(ends)])  7.48 us
  transfers between devices with their start and end apart: 13, of which 12 were waited for; matrix products, arithmetic and copies ran while one was open for 0% of the time, Pallas kernels for 0%

commit v1 on v0

--- a/solution.py
+++ b/solution.py
@@ -1,7 +1,426 @@
+import functools
+
 import jax
 import jax.numpy as jnp
 from jax import lax
+from jax.experimental import pallas as pl
+from jax.experimental.pallas import tpu as pltpu
 from jax.sharding import PartitionSpec as P
+
+MESH = pl.DeviceIdType.MESH
+VMEM = pl.BlockSpec(memory_space=pltpu.VMEM)
+AXES = ("gz", "gy", "col")
+
+
+def place():
+    return [lax.axis_index(a) for a in AXES], [lax.axis_size(a) for a in AXES]
+
+
+def remote(src, dst, send, recv, target):
+    return pltpu.make_async_remote_copy(
+        src_ref=src, dst_ref=dst, send_sem=send, recv_sem=recv,
+        device_id=target, device_id_type=MESH,
+    )
+
+
+def greet(target):
+    pl.semaphore_signal(
+        pltpu.get_barrier_semaphore(), inc=1, device_id=target, device_id_type=MESH
+    )
+
+
+def gather_kernel(vol, ext, own_sem, cs, cr, zs, zr, ys, yr):
+    (gz, gy, col), (nz, ny, nc) = place()
+    bz, by = vol.shape[:2]
+    has_z = (gz > 0, gz < nz - 1)
+    has_y = (gy > 0, gy < ny - 1)
+    z_dev = ((gz - 1, gy, col), (gz + 1, gy, col))
+    y_dev = ((gz, gy - 1, col), (gz, gy + 1, col))
+    rows_z, rows_y = pl.ds(1, bz), pl.ds(1, by)
+
+    own = pltpu.make_async_copy(vol, ext.at[rows_z, rows_y, col], own_sem)
+    own.start()
+    for j in range(1, nc):
+        greet((gz, gy, lax.rem(col + j, nc)))
+    count = nc - 1
+    for d in range(2):
+        pl.when(has_z[d])(functools.partial(greet, z_dev[d]))
+        pl.when(has_y[d])(functools.partial(greet, y_dev[d]))
+        count = count + has_z[d].astype(jnp.int32) + has_y[d].astype(jnp.int32)
+    pl.semaphore_wait(pltpu.get_barrier_semaphore(), count)
+
+    def col_copy(j, z, block, target):
+        return remote(vol.at[z], ext.at[1 + z, rows_y, block], cs.at[j, z], cr.at[j, z], target)
+
+    def z_copy(j, block, d):
+        src, dst = ((1, bz + 1), (bz, 0))[d]
+        return remote(
+            ext.at[src, rows_y, block], ext.at[dst, rows_y, block],
+            zs.at[j, d], zr.at[j, d], z_dev[d],
+        )
+
+    def y_copy(j, block, d, part):
+        src, dst = ((1, by + 1), (by, 0))[d]
+        z = (rows_z, pl.ds(0, 1), pl.ds(bz + 1, 1))[part]
+        return remote(
+            ext.at[z, src, block], ext.at[z, dst, block],
+            ys.at[j, d, part], yr.at[j, d, part], y_dev[d],
+        )
+
+    for j in range(1, nc):
+        for z in range(bz):
+            col_copy(j, z, col, (gz, gy, lax.rem(col + j, nc))).start()
+
+    for d in range(2):
+        @pl.when(jnp.logical_not(has_z[d]))
+        def _(d=d):
+            ext[(0, bz + 1)[d]] = jnp.zeros(ext.shape[1:], ext.dtype)
+
+        @pl.when(jnp.logical_not(has_y[d]))
+        def _(d=d):
+            for z in range(bz + 2):
+                ext[z, (0, by + 1)[d]] = jnp.zeros(ext.shape[2:], ext.dtype)
+
+    own.wait()
+    blocks = [col] + [lax.rem(col + nc - j, nc) for j in range(1, nc)]
+    for j, block in enumerate(blocks):
+        order = [0] + [z for z in range(bz) if z > 0]
+        for z in order:
+            if j > 0:
+                col_copy(j, z, block, (gz, gy, block)).wait_recv()
+            if z == 0:
+                pl.when(has_z[0])(lambda j=j, block=block: z_copy(j, block, 0).start())
+            if z == bz - 1:
+                pl.when(has_z[1])(lambda j=j, block=block: z_copy(j, block, 1).start())
+        for d in range(2):
+            pl.when(has_y[d])(lambda j=j, block=block, d=d: y_copy(j, block, d, 0).start())
+    for j, block in enumerate(blocks):
+        for h in range(2):
+            @pl.when(has_z[h])
+            def _(j=j, block=block, h=h):
+                z_copy(j, block, 1 - h).wait_recv()
+                for d in range(2):
+                    pl.when(has_y[d])(lambda: y_copy(j, block, d, 1 + h).start())
+    for j, block in enumerate(blocks):
+        if j > 0:
+            for z in range(bz):
+                col_copy(j, z, block, (gz, gy, block)).wait_send()
+        for d in range(2):
+            pl.when(has_z[d])(lambda j=j, block=block, d=d: z_copy(j, block, d).wait_send())
+
+            @pl.when(has_y[d])
+            def _(j=j, block=block, d=d):
+                y_copy(j, block, d, 0).wait_send()
+                y_copy(j, block, 1 - d, 0).wait_recv()
+                for h in range(2):
+                    @pl.when(has_z[h])
+                    def _(h=h):
+                        y_copy(j, block, d, 1 + h).wait_send()
+                        y_copy(j, block, 1 - d, 1 + h).wait_recv()
+
+
+def gathered_brick(volume):
+    bz, by, ch, bx = volume.shape
+    nc = lax.axis_size("col")
+    dma = pltpu.SemaphoreType.DMA
+    return pl.pallas_call(
+        gather_kernel,
+        out_shape=jax.ShapeDtypeStruct((bz + 2, by + 2, nc, ch, bx), volume.dtype),
+        in_specs=[pl.BlockSpec(memory_space=pl.ANY)],
+        out_specs=VMEM,
+        scratch_shapes=[
+            dma, dma((nc, bz)), dma((nc, bz)), dma((nc, 2)), dma((nc, 2)),
+            dma((nc, 2, 3)), dma((nc, 2, 3)),
+        ],
+        compiler_params=pltpu.CompilerParams(
+            collective_id=0, has_side_effects=True, vmem_limit_bytes=32 << 20
+        ),
+        name="gather_brick",
+    )(volume)
+
+
+def conv_kernel(ext, weights, out, total):
+    tap = pl.program_id(0)
+    dz, dy, dx = tap // 9, lax.rem(tap // 3, 3), lax.rem(tap, 3)
+    bz, by, bx, wide = out.shape
+    channels = weights.shape[-1]
+    matrix = weights[0].reshape(2 * wide, channels)
+    for z in range(bz):
+        cells = jnp.concatenate(
+            [ext[dz + z, dy + y].reshape(channels, bx) for y in range(by)], axis=1
+        )
+        product = jnp.dot(matrix, cells, preferred_element_type=jnp.float32)
+
+        @pl.when(tap < 3)
+        def _():
+            total[dx, z] = product
+
+        @pl.when(tap >= 3)
+        def _():
+            total[dx, z] += product
+
+    @pl.when(tap == pl.num_programs(0) - 1)
+    def _():
+        step = min(wide, 128)
+        lane = lax.broadcasted_iota(jnp.int32, (step, bx), 1)
+
+        def summed(z, first, y):
+            rows, xs = pl.ds(first, step), pl.ds(y * bx, bx)
+            before = pltpu.roll(total[0, z, rows, xs], 1, 1)
+            after = pltpu.roll(total[2, z, rows, xs], bx - 1, 1)
+            return (
+                total[1, z, rows, xs]
+                + jnp.where(lane == 0, 0.0, before)
+                + jnp.where(lane == bx - 1, 0.0, after)
+            )
+
+        for z in range(bz):
+            for y in range(by):
+                for first in range(0, wide, step):
+                    gate = summed(z, first, y)
+                    value = summed(z, wide + first, y)
+                    gated = gate / (1.0 + jnp.exp(-gate)) * value
+                    out[z, y, :, pl.ds(first, step)] = gated.T.astype(out.dtype)
+
+
+def gated_conv(ext, weights, brick):
+    bz, by = brick
+    taps, two, wide, channels = weights.shape
+    bx = ext.shape[-1]
+    return pl.pallas_call(
+        conv_kernel,
+        grid=(taps,),
+        out_shape=jax.ShapeDtypeStruct((bz, by, bx, wide), jnp.bfloat16),
+        in_specs=[
+            pl.BlockSpec(ext.shape, lambda t: (0,) * 5),
+            pl.BlockSpec((1, two, wide, channels), lambda t: (t, 0, 0, 0)),
+        ],
+        out_specs=pl.BlockSpec((bz, by, bx, wide), lambda t: (0,) * 4),
+        scratch_shapes=[pltpu.VMEM((3, bz, two * wide, by * bx), jnp.float32)],
+        compiler_params=pltpu.CompilerParams(vmem_limit_bytes=48 << 20),
+        cost_estimate=pl.CostEstimate(
+            flops=2 * taps * two * wide * channels * bz * by * bx,
+            bytes_accessed=2 * weights.size + 2 * ext.size,
+            transcendentals=bz * by * bx * wide,
+        ),
+        name="gated_conv",
+    )(ext, weights)
+
+
+def project_kernel(gated, proj, ext, other, rows, cs, cr, zs, zr, ys, yr):
+    (gz, gy, col), (nz, ny, nc) = place()
+    bz, by, bx, wide = gated.shape
+    piece = bx // nc
+    z_dev = ((lax.rem(gz + nz - 1, nz), gy, col), (lax.rem(gz + 1, nz), gy, col))
+    y_dev = ((gz, lax.rem(gy + ny - 1, ny), col), (gz, lax.rem(gy + 1, ny), col))
+    for j in range(1, nc):
+        greet((gz, gy, lax.rem(col + j, nc)))
+    for d in range(2):
+        greet(z_dev[d])
+        greet(y_dev[d])
+    pl.semaphore_wait(pltpu.get_barrier_semaphore(), nc + 3)
+
+    def col_copy(j):
+        target = lax.rem(col + j, nc)
+        xs = pl.ds(pl.multiple_of(target * piece, piece), piece)
+        return remote(
+            gated.at[:, :, xs], other.at[j], cs.at[j], cr.at[j], (gz, gy, target)
+        )
+
+    for j in range(1, nc):
+        col_copy(j).start()
+
+    def projected(cells, block):
+        return jnp.dot(
+            cells.reshape(bz * by * piece, wide),
+            proj[pl.ds(pl.multiple_of(block * wide, wide), wide), :],
+            preferred_element_type=jnp.float32,
+        )
+
+    total = projected(
+        gated[:, :, pl.ds(pl.multiple_of(col * piece, piece), piece), :], col
+    )
+    for j in range(1, nc):
+        col_copy(j).wait_recv()
+        total += projected(other[j], lax.rem(col + nc - j, nc))
+
+    bands, quads, lanes = 4, piece // 4, ext.shape[-1]
+    for b in range(4):
+        rows[b] = total[:, b * lanes : (b + 1) * lanes]
+    width = lanes // 4
+    slot = lax.broadcasted_iota(jnp.int32, (quads, lanes), 1) // width
+    for z in range(bz):
+        for y in range(by):
+            first = (z * by + y) * piece
+            for b in range(4):
+                parts = [
+                    rows[b, pl.ds(first + r, quads, stride=4), :]
+                    for r in range(4)
+                ]
+                for q in range(bands):
+                    packed = None
+                    for r in range(4):
+                        shift = ((r - q) * width) % lanes
+                        part = pltpu.roll(parts[r], shift, 1) if shift else parts[r]
+                        packed = part if packed is None else jnp.where(slot == r, part, packed)
+                    ext[2 + z, 2 + y, b // 2, b % 2, q] = packed.astype(ext.dtype)
+
+    def moves(n):
+        return ((n, 0, True, 1), (n + 1, 1, False, 1), (2, n + 2, False, 0))
+
+    def band(high):
+        return pl.ds(1, 1) if high else pl.ds(0, 2)
+
+    def z_copy(k):
+        src, dst, high, d = moves(bz)[k]
+        inner = pl.ds(2, by)
+        return remote(
+            ext.at[src, inner, band(high)], ext.at[dst, inner, band(high)],
+            zs.at[k], zr.at[k], z_dev[d],
+        )
+
+    groups = ((2, bz, False), (0, 1, True), (1, 1, False), (bz + 2, 1, False))
+
+    def y_copy(k, g):
+        src, dst, high, d = moves(by)[k]
+        start, size, z_high = groups[g]
+        zr_ = pl.ds(start, size)
+        return remote(
+            ext.at[zr_, src, band(z_high), band(high)],
+            ext.at[zr_, dst, band(z_high), band(high)],
+            ys.at[k, g], yr.at[k, g], y_dev[d],
+        )
+
+    for k in (1, 2, 0):
+        z_copy(k).start()
+    for k in (1, 2, 0):
+        y_copy(k, 0).start()
+    for m in (1, 2, 0):
+        z_copy(m).wait_recv()
+        for k in (1, 2, 0):
+            y_copy(k, m + 1).start()
+    for j in range(1, nc):
+        col_copy(j).wait_send()
+    for k in range(3):
+        z_copy(k).wait_send()
+        for g in range(4):
+            y_copy(k, g).wait_send()
+    for k in range(3):
+        for g in range(4):
+            y_copy(k, g).wait_recv()
+
+
+def projected_brick(gated, proj):
+    bz, by, bx, wide = gated.shape
+    nc = lax.axis_size("col")
+    piece, lanes = bx // nc, proj.shape[1] // 4
+    dma = pltpu.SemaphoreType.DMA
+    return pl.pallas_call(
+        project_kernel,
+        out_shape=jax.ShapeDtypeStruct(
+            (bz + 3, by + 3, 2, 2, 4, piece // 4, lanes), jnp.bfloat16
+        ),
+        in_specs=[VMEM, VMEM],
+        out_specs=VMEM,
+        scratch_shapes=[
+            pltpu.VMEM((nc, bz, by, piece, wide), gated.dtype),
+            pltpu.VMEM((4, bz * by * piece, lanes), jnp.float32),
+            dma((nc,)), dma((nc,)), dma((3,)), dma((3,)), dma((3, 4)), dma((3, 4)),
+        ],
+        compiler_params=pltpu.CompilerParams(
+            collective_id=1, has_side_effects=True, vmem_limit_bytes=32 << 20
+        ),
+        name="project",
+    )(gated, proj)
+
+
+def coarse_lift(low, high):
+    count = len(high)
+    even = [low[i] - 0.25 * (high[i - 1] + high[i]) for i in range(1, count)]
+    odd = [high[i + 1] + 0.5 * (even[i] + even[i + 1]) for i in range(count - 2)]
+    result = []
+    for i in range(count - 2):
+        result += [odd[i], even[i + 1]]
+    return result
+
+
+def fine_lift(low, high):
+    count = len(high)
+    even = [low[i] - 0.25 * (high[i - 1] + high[i]) for i in range(1, count)]
+    result = []
+    for i in range(count - 2):
+        result += [even[i], high[i + 1] + 0.5 * (even[i] + even[i + 1])]
+    return result
+
+
+def synthesis_kernel(ext, out, middle, tiles):
+    nz, ny = ext.shape[:2]
+    for band in range(4):
+        def column(y, hz, hy):
+            return [
+                None if z == 0 and not hz else ext[z, y, hz, hy, band].astype(jnp.float32)
+                for z in range(nz)
+            ]
+
+        low = [
+            None if y == 0 else coarse_lift(column(y, 0, 0), column(y, 1, 0))
+            for y in range(ny)
+        ]
+        high = [coarse_lift(column(y, 0, 1), column(y, 1, 1)) for y in range(ny)]
+        for z in range(len(high[0])):
+            line = coarse_lift(
+                [None if part is None else part[z] for part in low],
+                [part[z] for part in high],
+            )
+            for y, cells in enumerate(line):
+                middle[band, z, y] = cells
+    mz, my = middle.shape[1:3]
+    low, high = [], []
+    for y in range(my):
+        low.append(fine_lift([middle[0, z, y] for z in range(mz)], [middle[2, z, y] for z in range(mz)]))
+        high.append(fine_lift([middle[1, z, y] for z in range(mz)], [middle[3, z, y] for z in range(mz)]))
+    quads, lanes = middle.shape[3:]
+    for z in range(out.shape[0]):
+        line = fine_lift([part[z] for part in low], [part[z] for part in high])
+        for y, cells in enumerate(line):
+            tiles[z, pl.ds(y * quads, quads), :] = cells
+        for quad in range(quads):
+            out[z, :, pl.ds(quad * lanes, lanes)] = tiles[z, pl.ds(quad, out.shape[1], stride=quads), :]
+
+
+def synthesized(ext):
+    nz, ny = ext.shape[:2]
+    quads, lanes = ext.shape[-2:]
+    fz, fy = 4 * (nz - 3), 4 * (ny - 3)
+    return pl.pallas_call(
+        synthesis_kernel,
+        out_shape=jax.ShapeDtypeStruct((fz, fy, quads * lanes), jnp.float32),
+        in_specs=[VMEM],
+        out_specs=VMEM,
+        scratch_shapes=[
+            pltpu.VMEM((4, 2 * (nz - 2), 2 * (ny - 2), quads, lanes), jnp.float32),
+            pltpu.VMEM((fz, fy * quads, lanes), jnp.float32),
+        ],
+        compiler_params=pltpu.CompilerParams(vmem_limit_bytes=32 << 20),
+        name="synthesis",
+    )(ext)
+
+
+def on_device_kernels(volume, conv_weight, proj_weight):
+    ext = gathered_brick(volume)
+    gated = gated_conv(ext, conv_weight, volume.shape[:2])
+    return synthesized(projected_brick(gated, proj_weight))
+
+
+def fits(volume, conv_weight, proj_weight):
+    bz, by, ch, bx = volume.shape
+    wide, piece = conv_weight.shape[2], bx // lax.axis_size("col")
+    return (
+        min(bz, by) >= 2
+        and min(lax.axis_size("gz"), lax.axis_size("gy")) >= 3
+        and ch % 16 == 0 and bx == 128 and wide % 128 == 0
+        and piece % 64 == 0 and proj_weight.shape[1] == 4 * 128
+    )
 
 
 def extended_2(cells, sides, width, closed):
@@ -64,6 +483,8 @@
 
 
 def on_device(volume, conv_weight, proj_weight):
+    if fits(volume, conv_weight, proj_weight):
+        return on_device_kernels(volume, conv_weight, proj_weight)
     out_width = conv_weight.shape[2]
     gathered = lax.all_gather(volume, "col", axis=2, tiled=True)
     extended = extended_2(gathered, (("gz", 0), ("gy", 1)), 1, False)

time: 204 us -> 127 us (0.62)
  Pallas kernels: 0 us -> 124 us
  waiting for transfers between devices: 80.5 us -> 0 us
  matrix products: 37.6 us -> 0 us
  local copies, waits for them, and re-layouts: 33.4 us -> 1.05 us
  starting transfers between devices: 21.4 us -> 0 us
  between operations: 13.7 us -> 0.04 us
  blocking collectives: 8.14 us -> 0 us
  other arithmetic: 8.12 us -> 0 us
    pallas_call x0 -> x4, Pallas kernels: none -> 124 us  [the longest x1 75.5 us: gated_conv(): pl.pallas_call(conv_kernel, grid=(taps,), out_shape=jax.ShapeDtypeStruct(...]
    ppermute x12 -> x0, waiting for transfers between devices: 54.7 us -> none  [the longest x6 41.2 us: extended_2(): lax.ppermute(tail, axis, [(i, (i + 1) % count) for i in range(ends)])]
    conv_general_dilated x1 -> x0, matrix products: 37.2 us -> none  [convolve(): lax.conv_general_dilated(brick_data[None], kernel, (1, 1, 1), ((0, 0), (0...]
    all_gather x1 -> x0, waiting for transfers between devices: 25.1 us -> none  [on_device(): gathered = lax.all_gather(volume, 'col', axis=2, tiled=True)]
    ppermute x12 -> x0, starting transfers between devices: 21.4 us -> none  [the longest x6 14 us: extended_2(): lax.ppermute(tail, axis, [(i, (i + 1) % count) for i in range(ends)])]
    unnamed x10 -> x4, local copies, waits for them, and re-layouts: 10.9 us -> 1.05 us
    all_to_all x1 -> x0, blocking collectives: 8.14 us -> none  [on_device(): lax.all_to_all(gated_values, 'col', split_axis=3, concat_axis=2, tiled=True)]
    conv_general_dilated x4 -> x0, local copies, waits for them, and re-layouts: 5.45 us -> none  [convolve(): lax.conv_general_dilated(brick_data[None], kernel, (1, 1, 1), ((0, 0), (0...]
  transfers between devices with their start and end apart: 13 -> 0, of which waited for: 12 -> 0; matrix products, arithmetic and copies ran while one was open for 0% -> 0% of each run, Pallas kernels for 0% -> 0%
where the time goes in v1:
time: 127 us; the launch traced here: 125 us
  Pallas kernels  124 us (98%)
    pallas_call x1, Pallas kernels, gated_conv(): pl.pallas_call(conv_kernel, grid=(taps,), out_shape=jax.ShapeDtypeStruct(...  75.5 us
    pallas_call x1, Pallas kernels, gathered_brick(): pl.pallas_call(gather_kernel, out_shape=jax.ShapeDtypeStruct((bz + 2, by...  24.6 us
    pallas_call x1, Pallas kernels, projected_brick(): pl.pallas_call(project_kernel, out_shape=jax.ShapeDtypeStruct((bz + 3, by...  22.8 us

profile of v1, /device:TPU:1, one launch (start us, length us, event | category | flops | bytes accessed | tf_op | source)
XLA Modules:
  0.0 125.5 jit_solution(4186652113563154398)
XLA Ops:
  0.0 0.0 copy-start.1
  0.0 1.0 copy-done.1
  1.0 24.6 %gather_brick.1.ext = bf16[4,4,2,512,128]{4,3,2,1,0:T(8,128)(2,1)S(1)} custom-call(bf16[2,2,512,128]{3,2,1,0:T(8,128)(2,1)S(1)} %copy-done.1), custom_call_target="tpu_custom_call" | custom-call | tf_op jit(solution)/shard_map/gather_brick/pallas_call | solution.py:126
  25.7 0.0 copy-start
  25.7 75.5 %gated_conv.1.gated = bf16[2,2,128,512]{3,2,1,0:T(8,128)(2,1)S(1)} custom-call(bf16[4,4,2,512,128]{4,3,2,1,0:T(8,128)(2,1)S(1)} %gather_brick.1.ext, bf16[27,2,512,1024]{3,2,1,0:T(8,128)(2,1)} %weights.1), custom_call_target="tpu_custom_call" | custom-call | flops 28991029248 | bytes 60817408 | tf_op jit(solution)/shard_map/gated_conv/pallas_call | solution.py:190
  101.2 0.0 copy-done
  101.2 22.8 %project.1.ext = bf16[5,5,2,2,4,16,128]{6,5,4,3,2,1,0:T(8,128)(2,1)S(1)} custom-call(bf16[2,2,128,512]{3,2,1,0:T(8,128)(2,1)S(1)} %gated_conv.1.gated, bf16[1024,512]{1,0:T(8,128)(2,1)S(1)} %copy-done), custom_call_target="tpu_custom_call" | custom-call | tf_op jit(solution)/shard_map/project/pallas_call | solution.py:318
  124.0 1.4 %synthesis.1 = f32[8,8,2048]{2,1,0:T(8,128)} custom-call(bf16[5,5,2,2,4,16,128]{6,5,4,3,2,1,0:T(8,128)(2,1)S(1)} %project.1.ext), custom_call_target="tpu_custom_call" | custom-call | tf_op jit(solution)/shard_map/synthesis/pallas_call | solution.py:395
Async XLA Ops:
  0.0 1.0 copy-start.1
  25.7 75.5 %copy-start = (bf16[1024,512]{1,0:T(8,128)(2,1)S(1)}, bf16[1024,512]{1,0:T(8,128)(2,1)}, u32[]{:S(2)}) copy-start(bf16[1024,512]{1,0:T(8,128)(2,1)} %proj.1) | copy-start | bytes 3145732

commit v2 on v1

--- a/solution.py
+++ b/solution.py
@@ -140,36 +140,38 @@
 
 
 def conv_kernel(ext, weights, out, total):
-    tap = pl.program_id(0)
-    dz, dy, dx = tap // 9, lax.rem(tap // 3, 3), lax.rem(tap, 3)
+    step_index = pl.program_id(0)
+    dz, dx = step_index // 3, lax.rem(step_index, 3)
     bz, by, bx, wide = out.shape
     channels = weights.shape[-1]
-    matrix = weights[0].reshape(2 * wide, channels)
-    for z in range(bz):
+
+    @pl.when(dz == 0)
+    def _():
+        total[dx] = jnp.zeros(total.shape[1:], total.dtype)
+
+    for dy in range(3):
         cells = jnp.concatenate(
-            [ext[dz + z, dy + y].reshape(channels, bx) for y in range(by)], axis=1
-        )
-        product = jnp.dot(matrix, cells, preferred_element_type=jnp.float32)
-
-        @pl.when(tap < 3)
-        def _():
-            total[dx, z] = product
-
-        @pl.when(tap >= 3)
-        def _():
-            total[dx, z] += product
-
-    @pl.when(tap == pl.num_programs(0) - 1)
+            [
+                ext[dz + z, dy + y].reshape(channels, bx)
+                for z in range(bz)
+                for y in range(by)
+            ],
+            axis=1,
+        )
+        matrix = weights[0, dy, 0].reshape(2 * wide, channels)
+        total[dx] += jnp.dot(matrix, cells, preferred_element_type=jnp.float32)
+
+    @pl.when(step_index == pl.num_programs(0) - 1)
     def _():
         step = min(wide, 128)
         lane = lax.broadcasted_iota(jnp.int32, (step, bx), 1)
 
         def summed(z, first, y):
-            rows, xs = pl.ds(first, step), pl.ds(y * bx, bx)
-            before = pltpu.roll(total[0, z, rows, xs], 1, 1)
-            after = pltpu.roll(total[2, z, rows, xs], bx - 1, 1)
+            rows, xs = pl.ds(first, step), pl.ds((z * by + y) * bx, bx)
+            before = pltpu.roll(total[0, rows, xs], 1, 1)
+            after = pltpu.roll(total[2, rows, xs], bx - 1, 1)
             return (
-                total[1, z, rows, xs]
+                total[1, rows, xs]
                 + jnp.where(lane == 0, 0.0, before)
                 + jnp.where(lane == bx - 1, 0.0, after)
             )
@@ -189,14 +191,16 @@
     bx = ext.shape[-1]
     return pl.pallas_call(
         conv_kernel,
-        grid=(taps,),
+        grid=(9,),
         out_shape=jax.ShapeDtypeStruct((bz, by, bx, wide), jnp.bfloat16),
         in_specs=[
             pl.BlockSpec(ext.shape, lambda t: (0,) * 5),
-            pl.BlockSpec((1, two, wide, channels), lambda t: (t, 0, 0, 0)),
+            pl.BlockSpec(
+                (1, 3, 1, two, wide, channels), lambda t: (t // 3, 0, t % 3, 0, 0, 0)
+            ),
         ],
         out_specs=pl.BlockSpec((bz, by, bx, wide), lambda t: (0,) * 4),
-        scratch_shapes=[pltpu.VMEM((3, bz, two * wide, by * bx), jnp.float32)],
+        scratch_shapes=[pltpu.VMEM((3, two * wide, bz * by * bx), jnp.float32)],
         compiler_params=pltpu.CompilerParams(vmem_limit_bytes=48 << 20),
         cost_estimate=pl.CostEstimate(
             flops=2 * taps * two * wide * channels * bz * by * bx,
@@ -204,7 +208,7 @@
             transcendentals=bz * by * bx * wide,
         ),
         name="gated_conv",
-    )(ext, weights)
+    )(ext, weights.reshape((3, 3, 3) + weights.shape[1:]))
 
 
 def project_kernel(gated, proj, ext, other, rows, cs, cr, zs, zr, ys, yr):

time: 127 us -> 86.9 us (0.68)
  Pallas kernels: 124 us -> 84.8 us
    pallas_call x1, Pallas kernels: 75.5 us -> 35.9 us  [gated_conv(): pl.pallas_call(conv_kernel, grid=(9,), out_shape=jax.ShapeDtypeStruct((bz...]
where the time goes in v2:
time: 86.9 us; the launch traced here: 85.9 us
  Pallas kernels  84.8 us (98%)
  local copies, waits for them, and re-layouts  1.05 us (1%)
    pallas_call x1, Pallas kernels, gated_conv(): pl.pallas_call(conv_kernel, grid=(9,), out_shape=jax.ShapeDtypeStruct((bz...  35.9 us
    pallas_call x1, Pallas kernels, gathered_brick(): pl.pallas_call(gather_kernel, out_shape=jax.ShapeDtypeStruct((bz + 2, by...  24.6 us
    pallas_call x1, Pallas kernels, projected_brick(): pl.pallas_call(project_kernel, out_shape=jax.ShapeDtypeStruct((bz + 3, by...  22.8 us

profile of v2, /device:TPU:1, one launch (start us, length us, event | category | flops | bytes accessed | tf_op | source)
XLA Modules:
  0.0 85.9 jit_solution(7544241310900641442)
XLA Ops:
  0.0 0.0 copy-start.1
  0.0 1.0 %copy-done.1 = bf16[2,2,512,128]{3,2,1,0:T(8,128)(2,1)S(1)} copy-done((bf16[2,2,512,128]{3,2,1,0:T(8,128)(2,1)S(1)}, bf16[2,2,512,128]{3,2,1,0:T(8,128)(2,1)}, u32[]{:S(2)}) %copy-start.1) | copy-done | bytes 524312
  1.0 24.6 %gather_brick.1.ext = bf16[4,4,2,512,128]{4,3,2,1,0:T(8,128)(2,1)S(1)} custom-call(bf16[2,2,512,128]{3,2,1,0:T(8,128)(2,1)S(1)} %copy-done.1), custom_call_target="tpu_custom_call" | custom-call | tf_op jit(solution)/shard_map/gather_brick/pallas_call | solution.py:126
  25.7 0.0 copy-start
  25.7 35.9 %gated_conv.1.gated = bf16[2,2,128,512]{3,2,1,0:T(8,128)(2,1)S(1)} custom-call(bf16[4,4,2,512,128]{4,3,2,1,0:T(8,128)(2,1)S(1)} %gather_brick.1.ext, bf16[3,3,3,2,512,1024]{5,4,3,2,1,0:T(8,128)(2,1)} %bitcast.1), custom_call_target="tpu_custom_call" | custom-call | flops 28991029248 | bytes 60817408 | tf_op jit(solution)/shard_map/gated_conv/pallas_call | solution.py:192
  61.6 0.0 copy-done
  61.6 22.8 %project.1.ext = bf16[5,5,2,2,4,16,128]{6,5,4,3,2,1,0:T(8,128)(2,1)S(1)} custom-call(bf16[2,2,128,512]{3,2,1,0:T(8,128)(2,1)S(1)} %gated_conv.1.gated, bf16[1024,512]{1,0:T(8,128)(2,1)S(1)} %copy-done), custom_call_target="tpu_custom_call" | custom-call | tf_op jit(solution)/shard_map/project/pallas_call | solution.py:322
  84.4 1.4 %synthesis.1 = f32[8,8,2048]{2,1,0:T(8,128)} custom-call(bf16[5,5,2,2,4,16,128]{6,5,4,3,2,1,0:T(8,128)(2,1)S(1)} %project.1.ext), custom_call_target="tpu_custom_call" | custom-call | tf_op jit(solution)/shard_map/synthesis/pallas_call | solution.py:399
Async XLA Ops:
  0.0 1.0 %copy-start.1 = (bf16[2,2,512,128]{3,2,1,0:T(8,128)(2,1)S(1)}, bf16[2,2,512,128]{3,2,1,0:T(8,128)(2,1)}, u32[]{:S(2)}) copy-start(bf16[2,2,512,128]{3,2,1,0:T(8,128)(2,1)} %vol.1) | copy-start | bytes 1572868
  25.7 35.9 %copy-start = (bf16[1024,512]{1,0:T(8,128)(2,1)S(1)}, bf16[1024,512]{1,0:T(8,128)(2,1)}, u32[]{:S(2)}) copy-start(bf16[1024,512]{1,0:T(8,128)(2,1)} %proj.1) | copy-start | bytes 3145732

commit v3 on v2

--- a/solution.py
+++ b/solution.py
@@ -224,36 +224,61 @@
         greet(y_dev[d])
     pl.semaphore_wait(pltpu.get_barrier_semaphore(), nc + 3)
 
-    def col_copy(j):
+    def col_copy(j, z):
         target = lax.rem(col + j, nc)
         xs = pl.ds(pl.multiple_of(target * piece, piece), piece)
         return remote(
-            gated.at[:, :, xs], other.at[j], cs.at[j], cr.at[j], (gz, gy, target)
-        )
-
-    for j in range(1, nc):
-        col_copy(j).start()
+            gated.at[z, :, xs], other.at[j, z], cs.at[j, z], cr.at[j, z], (gz, gy, target)
+        )
+
+    for z in range(bz):
+        for j in range(1, nc):
+            col_copy(j, z).start()
 
     def projected(cells, block):
         return jnp.dot(
-            cells.reshape(bz * by * piece, wide),
+            cells.reshape(by * piece, wide),
             proj[pl.ds(pl.multiple_of(block * wide, wide), wide), :],
             preferred_element_type=jnp.float32,
         )
 
-    total = projected(
-        gated[:, :, pl.ds(pl.multiple_of(col * piece, piece), piece), :], col
-    )
-    for j in range(1, nc):
-        col_copy(j).wait_recv()
-        total += projected(other[j], lax.rem(col + nc - j, nc))
-
     bands, quads, lanes = 4, piece // 4, ext.shape[-1]
-    for b in range(4):
-        rows[b] = total[:, b * lanes : (b + 1) * lanes]
     width = lanes // 4
     slot = lax.broadcasted_iota(jnp.int32, (quads, lanes), 1) // width
+    def moves(n):
+        return ((n, 0, True, 1), (n + 1, 1, False, 1), (2, n + 2, False, 0))
+
+    def band(high):
+        return pl.ds(1, 1) if high else pl.ds(0, 2)
+
+    def z_copy(k):
+        src, dst, high, d = moves(bz)[k]
+        inner = pl.ds(2, by)
+        return remote(
+            ext.at[src, inner, band(high)], ext.at[dst, inner, band(high)],
+            zs.at[k], zr.at[k], z_dev[d],
+        )
+
+    groups = ((2, bz, False), (0, 1, True), (1, 1, False), (bz + 2, 1, False))
+
+    def y_copy(k, g):
+        src, dst, high, d = moves(by)[k]
+        start, size, z_high = groups[g]
+        zr_ = pl.ds(start, size)
+        return remote(
+            ext.at[zr_, src, band(z_high), band(high)],
+            ext.at[zr_, dst, band(z_high), band(high)],
+            ys.at[k, g], yr.at[k, g], y_dev[d],
+        )
+
     for z in range(bz):
+        xs = pl.ds(pl.multiple_of(col * piece, piece), piece)
+        total = projected(gated[z, :, xs, :], col)
+        for j in range(1, nc):
+            col_copy(j, z).wait_recv()
+            total += projected(other[j, z], lax.rem(col + nc - j, nc))
+        for b in range(4):
+            rows[b, pl.ds(z * by * piece, by * piece), :] = total[:, b * lanes : (b + 1) * lanes]
         for y in range(by):
             first = (z * by + y) * piece
             for b in range(4):
@@ -268,35 +293,10 @@
                         part = pltpu.roll(parts[r], shift, 1) if shift else parts[r]
                         packed = part if packed is None else jnp.where(slot == r, part, packed)
                     ext[2 + z, 2 + y, b // 2, b % 2, q] = packed.astype(ext.dtype)
-
-    def moves(n):
-        return ((n, 0, True, 1), (n + 1, 1, False, 1), (2, n + 2, False, 0))
-
-    def band(high):
-        return pl.ds(1, 1) if high else pl.ds(0, 2)
-
-    def z_copy(k):
-        src, dst, high, d = moves(bz)[k]
-        inner = pl.ds(2, by)
-        return remote(
-            ext.at[src, inner, band(high)], ext.at[dst, inner, band(high)],
-            zs.at[k], zr.at[k], z_dev[d],
-        )
-
-    groups = ((2, bz, False), (0, 1, True), (1, 1, False), (bz + 2, 1, False))
-
-    def y_copy(k, g):
-        src, dst, high, d = moves(by)[k]
-        start, size, z_high = groups[g]
-        zr_ = pl.ds(start, size)
-        return remote(
-            ext.at[zr_, src, band(z_high), band(high)],
-            ext.at[zr_, dst, band(z_high), band(high)],
-            ys.at[k, g], yr.at[k, g], y_dev[d],
-        )
-
-    for k in (1, 2, 0):
-        z_copy(k).start()
+        for k in (1, 2, 0):
+            if moves(bz)[k][0] == 2 + z:
+                z_copy(k).start()
+
     for k in (1, 2, 0):
         y_copy(k, 0).start()
     for m in (1, 2, 0):
@@ -304,7 +304,8 @@
         for k in (1, 2, 0):
             y_copy(k, m + 1).start()
     for j in range(1, nc):
-        col_copy(j).wait_send()
+        for z in range(bz):
+            col_copy(j, z).wait_send()
     for k in range(3):
         z_copy(k).wait_send()
         for g in range(4):
@@ -329,7 +330,7 @@
         scratch_shapes=[
             pltpu.VMEM((nc, bz, by, piece, wide), gated.dtype),
             pltpu.VMEM((4, bz * by * piece, lanes), jnp.float32),
-            dma((nc,)), dma((nc,)), dma((3,)), dma((3,)), dma((3, 4)), dma((3, 4)),
+            dma((nc, bz)), dma((nc, bz)), dma((3,)), dma((3,)), dma((3, 4)), dma((3, 4)),
         ],
         compiler_params=pltpu.CompilerParams(
             collective_id=1, has_side_effects=True, vmem_limit_bytes=32 << 20

time: 86.9 us -> 86.4 us (level); the launches traced: 85.9 us -> 86.2 us
  no operation moved by 1% of the time
where the time goes in v3:
time: 86.4 us; the launch traced here: 86.2 us
  Pallas kernels  85.1 us (98%)
  local copies, waits for them, and re-layouts  1.05 us (1%)
    pallas_call x1, Pallas kernels, gated_conv(): pl.pallas_call(conv_kernel, grid=(9,), out_shape=jax.ShapeDtypeStruct((bz...  35.9 us
    pallas_call x1, Pallas kernels, gathered_brick(): pl.pallas_call(gather_kernel, out_shape=jax.ShapeDtypeStruct((bz + 2, by...  24.6 us
    pallas_call x1, Pallas kernels, projected_brick(): pl.pallas_call(project_kernel, out_shape=jax.ShapeDtypeStruct((bz + 3, by...  23.2 us

profile of v3, /device:TPU:1, one launch (start us, length us, event | category | flops | bytes accessed | tf_op | source)
XLA Modules:
  0.0 86.2 jit_solution(2119534374513468975)
XLA Ops:
  0.0 0.0 copy-start.1
  0.0 1.0 %copy-done.1 = bf16[2,2,512,128]{3,2,1,0:T(8,128)(2,1)S(1)} copy-done((bf16[2,2,512,128]{3,2,1,0:T(8,128)(2,1)S(1)}, bf16[2,2,512,128]{3,2,1,0:T(8,128)(2,1)}, u32[]{:S(2)}) %copy-start.1) | copy-done | bytes 524312
  1.0 24.6 %gather_brick.1.ext = bf16[4,4,2,512,128]{4,3,2,1,0:T(8,128)(2,1)S(1)} custom-call(bf16[2,2,512,128]{3,2,1,0:T(8,128)(2,1)S(1)} %copy-done.1), custom_call_target="tpu_custom_call" | custom-call | tf_op jit(solution)/shard_map/gather_brick/pallas_call | solution.py:126
  25.7 0.0 copy-start
  25.7 35.9 %gated_conv.1.gated = bf16[2,2,128,512]{3,2,1,0:T(8,128)(2,1)S(1)} custom-call(bf16[4,4,2,512,128]{4,3,2,1,0:T(8,128)(2,1)S(1)} %gather_brick.1.ext, bf16[3,3,3,2,512,1024]{5,4,3,2,1,0:T(8,128)(2,1)} %bitcast.1), custom_call_target="tpu_custom_call" | custom-call | flops 28991029248 | bytes 60817408 | tf_op jit(solution)/shard_map/gated_conv/pallas_call | solution.py:192
  61.6 0.0 copy-done
  61.6 23.2 %project.1.ext = bf16[5,5,2,2,4,16,128]{6,5,4,3,2,1,0:T(8,128)(2,1)S(1)} custom-call(bf16[2,2,128,512]{3,2,1,0:T(8,128)(2,1)S(1)} %gated_conv.1.gated, bf16[1024,512]{1,0:T(8,128)(2,1)S(1)} %copy-done), custom_call_target="tpu_custom_call" | custom-call | tf_op jit(solution)/shard_map/project/pallas_call | solution.py:323
  84.8 1.4 %synthesis.1 = f32[8,8,2048]{2,1,0:T(8,128)} custom-call(bf16[5,5,2,2,4,16,128]{6,5,4,3,2,1,0:T(8,128)(2,1)S(1)} %project.1.ext), custom_call_target="tpu_custom_call" | custom-call | tf_op jit(solution)/shard_map/synthesis/pallas_call | solution.py:400
Async XLA Ops:
  0.0 1.0 %copy-start.1 = (bf16[2,2,512,128]{3,2,1,0:T(8,128)(2,1)S(1)}, bf16[2,2,512,128]{3,2,1,0:T(8,128)(2,1)}, u32[]{:S(2)}) copy-start(bf16[2,2,512,128]{3,2,1,0:T(8,128)(2,1)} %vol.1) | copy-start | bytes 1572868
  25.7 35.9 %copy-start = (bf16[1024,512]{1,0:T(8,128)(2,1)S(1)}, bf16[1024,512]{1,0:T(8,128)(2,1)}, u32[]{:S(2)}) copy-start(bf16[1024,512]{1,0:T(8,128)(2,1)} %proj.1) | copy-start | bytes 3145732
